TPU v7x, 32 devices: a whole 2x2x4 slice. The times are simulated.
32 devices in a mesh: rep: 2 (over y), fsdp: 8 (over z, core), adapt: 2 (over x), sub: 1.
Axes of the slice: x: 2, y: 2, z: 4, core: 2. Of those that a mesh axis runs over, the one named last changes fastest.
Arguments:
- tokens: bfloat16 [2, 2048, 8192], P('adapt', ('rep', 'fsdp', 'sub')), parts along dimension 1, may hold values from -6 to 6
- frozen_key_weight: bfloat16 [8192, 512], P('fsdp'), may hold values from -0.0625 to 0.0625
- adapter_down_maps: float32 [2, 8, 8192, 16], P('adapt', 'rep', 'fsdp'), parts along dimension 1, may hold values from -0.0625 to 0.0625
- adapter_up_maps: float32 [2, 8, 16, 512], P('adapt', 'rep'), parts along dimension 1, may hold values from -0.9 to 0.9
- tenant_of_block: int32 [2, 32], P('adapt', ('rep', 'fsdp', 'sub')), parts along dimension 1, may hold values from 0 to 3, as said below
- adapter_of_tenant: int32 [2, 8], P('adapt', 'rep'), parts along dimension 1, may hold values from 0 to 3
- cotangent: bfloat16 [2, 2048, 512], P('adapt', ('rep', 'fsdp', 'sub')), parts along dimension 1, may hold values from -6 to 6
Outputs:
- projected: bfloat16 [2, 2048, 512], P('adapt', ('rep', 'fsdp', 'sub')), parts along dimension 1
- token_input_gradient: bfloat16 [2, 2048, 8192], P('adapt', ('rep', 'fsdp', 'sub')), parts along dimension 1
- down_map_gradient: float32 [2, 8, 8192, 16], P('adapt', 'rep', ('fsdp', 'sub')), parts along dimension 1
- up_gradient_swapped: float32 [2, 8, 512, 16], P('adapt', 'rep', ('fsdp', 'sub')), parts along dimension 1
There are 2 independent parts, one for each index of `rep`. A program takes and returns all parts, laid end to end along the dimension named above; an argument that names none is the same for every part. Nothing has to cross between parts.
Inputs may be any that keep to these rules, and one draw needn't show every extreme that they name: `tenant_of_block`: in each group every tenant owns exactly 256 rows, that is 4 blocks.
All inputs are finite; a program needn't handle non-finite values.
Results may differ from a plain program's by a relative error of at most 0.001.
Values may be sent and summed in bfloat16 or wider, within the bound.
A program may use at most 64 MiB of HBM per device.

v0:
```python
import jax
import jax.numpy as jnp
from jax import lax
from jax.sharding import PartitionSpec as P

HIGH_PRECISION = lax.Precision.HIGHEST
adapter_scale = 2.0


def per_device(
    tokens,
    frozen_key_weight,
    adapter_down_maps,
    adapter_up_maps,
    tenant_of_block,
    adapter_of_tenant,
    cotangent,
):
    feats = tokens[0]
    grad_out = cotangent[0]
    owners = tenant_of_block[0]
    slot_table = adapter_of_tenant[0]
    rows = feats.shape[0]
    width = feats.shape[1]
    output_width = frozen_key_weight.shape[1]
    slot_count = adapter_down_maps.shape[1]
    adapter_rank_value = adapter_down_maps.shape[3]
    tenant_ids = jnp.arange(slot_table.shape[0], dtype=jnp.int32)
    slot_block = jnp.sum(
        jnp.where(owners[:, None] == tenant_ids[None, :], slot_table[None, :], 0), axis=1
    )
    slot_row = jnp.repeat(slot_block, rows // owners.shape[0])
    lanes = jnp.arange(slot_count * adapter_rank_value, dtype=jnp.int32) // adapter_rank_value
    slot_selection = (slot_row[:, None] == lanes[None, :]).astype(jnp.float32)
    complete_down_maps = lax.all_gather(adapter_down_maps, "fsdp", axis=2, tiled=True)[0]
    down_flattened = jnp.transpose(complete_down_maps, (1, 0, 2)).reshape(
        width, slot_count * adapter_rank_value
    )
    up_flattened = adapter_up_maps[0].reshape(slot_count * adapter_rank_value, output_width)
    feats32 = feats.astype(jnp.float32)
    low_rank_output = jnp.dot(feats32, down_flattened, precision=HIGH_PRECISION) * slot_selection
    whole_weight = lax.all_gather(frozen_key_weight, "fsdp", axis=0, tiled=True)
    frozen_output = jnp.dot(feats, whole_weight, preferred_element_type=jnp.float32)
    projected = (
        frozen_output
        + adapter_scale * jnp.dot(low_rank_output, up_flattened, precision=HIGH_PRECISION)
    ).astype(jnp.bfloat16)
    gradient_float32 = grad_out.astype(jnp.float32)
    low_rank_gradient = (
        adapter_scale
        * jnp.dot(gradient_float32, up_flattened.T, precision=HIGH_PRECISION)
        * slot_selection
    )
    up_gradient_flattened = adapter_scale * jnp.dot(
        gradient_float32.T, low_rank_output, precision=HIGH_PRECISION
    )
    grad_a_flat = jnp.dot(feats32.T, low_rank_gradient, precision=HIGH_PRECISION)
    back = jnp.dot(grad_out, whole_weight.T, preferred_element_type=jnp.float32)
    token_input_gradient = (
        back + jnp.dot(low_rank_gradient, down_flattened.T, precision=HIGH_PRECISION)
    ).astype(jnp.bfloat16)
    grad_a_local = jnp.transpose(
        grad_a_flat.reshape(width, slot_count, adapter_rank_value), (1, 0, 2)
    )[None]
    grad_b_local = jnp.transpose(
        up_gradient_flattened.reshape(output_width, slot_count, adapter_rank_value), (1, 0, 2)
    )[None]
    down_map_gradient, up_gradient_swapped = (
        lax.psum_scatter(grad_a_local, ("fsdp", "sub"), scatter_dimension=2, tiled=True),
        lax.psum_scatter(grad_b_local, ("fsdp", "sub"), scatter_dimension=2, tiled=True),
    )
    return (projected[None], token_input_gradient[None], down_map_gradient, up_gradient_swapped)


def solution(mesh):
    in_specs = (
        P("adapt", ("rep", "fsdp", "sub"), None),
        P("fsdp", None),
        P("adapt", "rep", "fsdp", None),
        P("adapt", "rep", None, None),
        P("adapt", ("rep", "fsdp", "sub")),
        P("adapt", "rep"),
        P("adapt", ("rep", "fsdp", "sub"), None),
    )
    out_specs = (
        P("adapt", ("rep", "fsdp", "sub"), None),
        P("adapt", ("rep", "fsdp", "sub"), None),
        P("adapt", "rep", ("fsdp", "sub"), None),
        P("adapt", "rep", ("fsdp", "sub"), None),
    )
    return jax.shard_map(
        per_device, mesh=mesh, in_specs=in_specs, out_specs=out_specs, check_vma=False
    )
```

profile of v0, /device:TPU:0, one launch (start us, length us, event | category | flops | bytes accessed | tf_op | source)
XLA Modules:
  0.0 203.3 jit_solution(10991898807495660832)
XLA Ops:
  7.2 0.0 copy-start
  7.2 0.0 all-gather.5.cloned.1.call-start
  7.2 0.7 all-gather.5.cloned.1.call-update
  7.9 0.0 reduce-scatter.7.cloned.1.call-start
  8.0 0.9 fusion.19
  8.8 0.1 broadcast_in_dim.34
  8.9 0.1 eq.34
  9.0 32.5 %all-gather.5.cloned.1.call-done = f32[1,4,8192,16]{2,3,1,0:T(8,128)} async-done(((f32[1,4,1024,16]{2,3,1,0:T(8,128)}), f32[1,4,8192,16]{2,3,1,0:T(8,128)}) %all-gather.5.cloned.1.call-update) | async-done | bytes 2097168 | tf_op jit(solution)/shard_map/all_gather | solution.py:35
  41.5 0.0 copy-done
  41.5 0.0 copy-start.3
  41.5 3.9 %fusion.11 = f32[128,64]{0,1:T(8,128)S(1)} fusion(f32[8192,64]{0,1:T(8,128)} %bitcast.55, bf16[1,128,8192]{2,1,0:T(8,128)(2,1)S(1)} %copy-done, s32[128]{0:T(128)S(1)} %eq.34, s32[64]{0:T(128)S(1)} %and_select_fusion), kind=kOutput, calls=%fused_computation.14 | convolution fusion | flops 805322752 | bytes 4227840 | tf_op jit(solution)/shard_map/dot_general | solution.py:41
  45.4 0.0 copy-done.3
  45.4 0.0 copy-start.5
  45.4 0.0 copy-start.4
  45.4 0.2 convolution_multiply_fusion.1
  45.6 0.4 copy-done.5
  46.0 0.4 copy.11
  46.4 1.2 reshape.35
  47.6 0.0 reduce-scatter.7.cloned.1.call-update
  47.6 0.0 all-gather.3.cloned.1.call-start
  47.6 0.7 all-gather.3.cloned.1.call-update
  48.3 0.0 reduce-scatter.5.cloned.1.call-start
  48.4 0.0 copy-done.4
  48.4 0.3 fusion.14
  48.6 2.3 %fusion.2 = f32[64,8192]{1,0:T(8,128)} fusion(f32[128,64]{0,1:T(8,128)S(1)} %fusion.14, bf16[1,128,8192]{2,1,0:T(8,128)(2,1)S(1)} %copy-done), kind=kOutput, calls=%fused_computation.3 | convolution fusion | flops 805306368 | bytes 4227072 | tf_op jit(solution)/shard_map/dot_general | solution.py:57
  51.0 0.0 reduce-scatter.5.cloned.1.call-update
  51.0 26.6 %reduce-scatter.7.cloned.1.call-done = f32[64,64]{1,0:T(8,128)} async-done(((f32[512,64]{1,0:T(8,128)}), f32[64,64]{1,0:T(8,128)}) %reduce-scatter.7.cloned.1.call-update) | async-done | bytes 16400
  77.6 0.9 reshape.36
  78.5 0.7 copy.12
  79.2 0.0 copy-start.6
  79.2 80.3 %all-gather.3.cloned.1.call-done = bf16[8192,512]{1,0:T(8,128)(2,1)} async-done(((bf16[1024,512]{1,0:T(8,128)(2,1)}), bf16[8192,512]{1,0:T(8,128)(2,1)}) %all-gather.3.cloned.1.call-update) | async-done | bytes 8388624 | tf_op jit(solution)/shard_map/all_gather | solution.py:42
  159.5 0.0 copy-start.1
  159.5 4.8 %fusion.6 = f32[128,512]{1,0:T(8,128)S(1)} fusion(bf16[8192,512]{1,0:T(8,128)(2,1)} %all-gather.3.cloned.1.call-done, bf16[1,128,8192]{2,1,0:T(8,128)(2,1)S(1)} %copy-done), kind=kOutput, calls=%fused_computation.7 | convolution fusion | flops 1073741824 | bytes 10747904 | tf_op jit(solution)/shard_map/dot_general | solution.py:43
  164.3 0.0 copy-done.6
  164.3 1.1 fusion.10
  165.4 0.0 copy-done.1
  165.4 0.0 copy-start.2
  165.4 2.8 %fusion.17 = f32[128,8192]{1,0:T(8,128)S(1)} fusion(bf16[8192,512]{1,0:T(8,128)(2,1)S(1)} %copy-done.1, bf16[1,128,512]{2,1,0:T(8,128)(2,1)S(1)} %copy-done.3), kind=kOutput, calls=%fused_computation.19 | convolution fusion | flops 1073741824 | bytes 12713984 | tf_op jit(solution)/shard_map/dot_general | solution.py:58
  168.2 0.0 copy-done.2
  168.2 4.8 %fusion.1 = bf16[1,128,8192]{2,1,0:T(8,128)(2,1)} fusion(f32[128,8192]{1,0:T(8,128)S(1)} %fusion.17, f32[128,64]{0,1:T(8,128)S(1)} %fusion.14, f32[8192,64]{0,1:T(8,128)S(1)} %bitcast.56), kind=kOutput, calls=%fused_computation.2 | convolution fusion | flops 807403520 | bytes 8421376 | tf_op jit(solution)/shard_map/dot_general | solution.py:60
  173.0 23.8 %reduce-scatter.5.cloned.1.call-done = f32[1,4,1024,16]{2,3,1,0:T(8,128)} async-done(((f32[1,4,8192,16]{2,3,1,0:T(8,128)}), f32[1,4,1024,16]{2,3,1,0:T(8,128)}) %reduce-scatter.5.cloned.1.call-update) | async-done | bytes 262160 | tf_op jit(solution)/shard_map/reduce_scatter | solution.py:69
  (1 shorter events, 0.0 us)
Async XLA Ops:
  7.2 34.3 %copy-start = (bf16[1,128,8192]{2,1,0:T(8,128)(2,1)S(1)}, bf16[1,128,8192]{2,1,0:T(8,128)(2,1)}, u32[]{:S(2)}) copy-start(bf16[1,128,8192]{2,1,0:T(8,128)(2,1)} %param.7) | copy-start | bytes 6291460
  7.2 34.3 %all-gather.5.cloned.1.call-start = ((), (), s32[]{:S(2)}) async-start(), calls=%async_computation.3 | async-start | bytes 2359296 | tf_op jit(solution)/shard_map/all_gather | solution.py:35
  7.9 69.7 %reduce-scatter.7.cloned.1.call-start = ((), (), s32[]{:S(2)}) async-start(), calls=%async_computation.5 | async-start | bytes 294912
  41.5 3.9 %copy-start.3 = (bf16[1,128,512]{2,1,0:T(8,128)(2,1)S(1)}, bf16[1,128,512]{2,1,0:T(8,128)(2,1)}, u32[]{:S(2)}) copy-start(bf16[1,128,512]{2,1,0:T(8,128)(2,1)} %param.13) | copy-start | bytes 393220
  45.4 0.6 copy-start.5
  45.4 3.0 %copy-start.4 = (f32[1,4,16,512]{3,2,1,0:T(8,128)S(1)}, f32[1,4,16,512]{3,2,1,0:T(8,128)}, u32[]{:S(2)}) copy-start(f32[1,4,16,512]{3,2,1,0:T(8,128)} %param.10) | copy-start | bytes 393220
  47.6 112.0 %all-gather.3.cloned.1.call-start = ((), (), s32[]{:S(2)}) async-start(), calls=%async_computation.2 | async-start | bytes 9437184 | tf_op jit(solution)/shard_map/all_gather | solution.py:42
  48.3 148.4 %reduce-scatter.5.cloned.1.call-start = ((), (), s32[]{:S(2)}) async-start(), calls=%async_computation.4 | async-start | bytes 2359296 | tf_op jit(solution)/shard_map/reduce_scatter | solution.py:69
  79.2 85.1 %copy-start.6 = (f32[128,64]{0,1:T(8,128)S(1)}, f32[128,64]{0,1:T(8,128)}, u32[]{:S(2)}) copy-start(f32[128,64]{0,1:T(8,128)} %copy-done.5) | copy-start | bytes 98308
  159.5 5.9 %copy-start.1 = (bf16[8192,512]{1,0:T(8,128)(2,1)S(1)}, bf16[8192,512]{1,0:T(8,128)(2,1)}, u32[]{:S(2)}) copy-start(bf16[8192,512]{1,0:T(8,128)(2,1)} %all-gather.3.cloned.1.call-done) | copy-start | bytes 25165828
  165.4 2.8 %copy-start.2 = (f32[1,4,8192,16]{2,3,1,0:T(8,128)S(1)}, f32[1,4,8192,16]{2,3,1,0:T(8,128)}, u32[]{:S(2)}) copy-start(f32[1,4,8192,16]{2,3,1,0:T(8,128)} %all-gather.5.cloned.1.call-done) | copy-start | bytes 6291460
Sparse Core Ops, SparseCore 0:
  9.6 31.7 all-gather.4
  47.7 29.8 reduce-scatter.6
  79.3 80.1 all-gather.2
  162.4 34.3 reduce-scatter.4
where the time goes:
time: 204 us; the launch traced here: 203 us
  waiting for transfers between devices  165 us (81%)
  matrix products  20.1 us (10%)
  between operations  13.9 us (7%)
  local copies, waits for them, and re-layouts  3.72 us (2%)
    all_gather x1, waiting for transfers between devices, per_device(): whole_weight = lax.all_gather(frozen_key_weight, 'fsdp', axis=0, tiled=True)  80.3 us
    all_gather x1, waiting for transfers between devices, per_device(): lax.all_gather(adapter_down_maps, 'fsdp', axis=2, tiled=True)[0]  32.5 us
    unnamed x5, waiting for transfers between devices  28 us
    reduce_scatter x1, waiting for transfers between devices, per_device(): lax.psum_scatter(grad_a_local, ('fsdp', 'sub'), scatter_dimension=2, tile...  23.8 us
    dot_general x1, matrix products, per_device(): jnp.dot(feats, whole_weight, preferred_element_type=jnp.float32)  4.78 us
    dot_general x1, matrix products, per_device(): jnp.dot(low_rank_gradient, down_flattened.T, precision=HIGH_PRECISION)  4.75 us
  transfers between devices with their start and end apart: 4, of which 4 were waited for; matrix products, arithmetic and copies ran while one was open for 9% of the time, Pallas kernels for 0%

commit v1 on v0

--- a/solution.py
+++ b/solution.py
@@ -1,6 +1,10 @@
+import functools
+
 import jax
 import jax.numpy as jnp
 from jax import lax
+from jax.experimental import pallas as pl
+from jax.experimental.pallas import tpu as pltpu
 from jax.sharding import PartitionSpec as P
 
 HIGH_PRECISION = lax.Precision.HIGHEST
@@ -72,7 +76,385 @@
     return (projected[None], token_input_gradient[None], down_map_gradient, up_gradient_swapped)
 
 
+CORES = 2
+MESH = pl.DeviceIdType.MESH
+bf16, f32 = jnp.bfloat16, jnp.float32
+
+
+def halves(x):
+    high = x.astype(bf16)
+    low = (x - high.astype(f32)).astype(bf16)
+    return high, low
+
+
+def dot_nn(a, b):
+    return lax.dot_general(a, b, (((1,), (0,)), ((), ())), preferred_element_type=f32)
+
+
+def dot_nt(a, b):
+    return lax.dot_general(a, b, (((1,), (1,)), ((), ())), preferred_element_type=f32)
+
+
+def pick(z, values):
+    out = values[-1]
+    for i in range(len(values) - 2, -1, -1):
+        out = jnp.where(z == i, values[i], out)
+    return out
+
+
+def step_kernel(
+    chips,
+    quarters,
+    rank,
+    tok_ref,
+    w_ref,
+    d_ref,
+    up_ref,
+    tenant_ref,
+    slot_ref,
+    cot_ref,
+    proj_ref,
+    tg_ref,
+    dg_ref,
+    ug_ref,
+    wbuf,
+    dbuf,
+    gbuf,
+    pbuf,
+    rup,
+    rdn,
+    ubuf,
+    urecv,
+    dlc,
+    acc,
+    lacc,
+    cw_s,
+    cw_r,
+    cd_s,
+    cd_r,
+    sd_s,
+    sd_r,
+    nb_s,
+    nb_r,
+    sb_s,
+    sb_r,
+    so_s,
+    so_r,
+    pr_s,
+    pr_r,
+    ch_s,
+    up_r,
+    dn_r,
+    ug_s,
+    ug_r,
+    cp_s,
+):
+    me = lax.axis_index("fsdp")
+    a = lax.axis_index("adapt")
+    r = lax.axis_index("rep")
+    n = chips * CORES
+    z, c = me // CORES, me % CORES
+    sib = z * CORES + (1 - c)
+    quarter = r * 2 + a
+    xq = r * 2 + (1 - a)
+    yq = (1 - r) * 2 + a
+    dq = (1 - r) * 2 + (1 - a)
+    rows, width = tok_ref.shape
+    depth = width // n
+    cols = d_ref.shape[0]
+    half = wbuf.shape[2] // 2
+    upper, lower = z < chips - 1, z > 0
+    SIB, XN, YN = {"fsdp": sib}, {"adapt": 1 - a}, {"rep": 1 - r}
+
+    def at(zz, cc=None):
+        return zz * CORES + (c if cc is None else cc)
+
+    def rc(src, dst, ss, rs, dev):
+        return pltpu.make_async_remote_copy(
+            src_ref=src, dst_ref=dst, send_sem=ss, recv_sem=rs, device_id=dev, device_id_type=MESH
+        )
+
+    sends = []
+
+    def send(cond, copy):
+        if cond is None:
+            copy.start()
+            sends.append((None, copy))
+        else:
+            pl.when(cond)(copy.start)
+            sends.append((cond, copy))
+
+    def landed(dst, rs):
+        rc(dst, dst, sb_s.at[0, 0], rs, SIB).wait_recv()
+
+    own_w = pltpu.make_async_copy(w_ref, wbuf.at[me], cp_s)
+    own_w.start()
+
+    barrier = pltpu.get_barrier_semaphore()
+    for i in range(1, n):
+        pl.semaphore_signal(barrier, inc=1, device_id={"fsdp": lax.rem(me + i, n)}, device_id_type=MESH)
+    pl.semaphore_signal(barrier, inc=1, device_id=XN, device_id_type=MESH)
+    pl.semaphore_signal(barrier, inc=1, device_id=YN, device_id_type=MESH)
+
+    d_hi, d_lo = halves(d_ref[...])
+    dbuf[me, :cols] = d_hi
+    dbuf[me, cols:] = d_lo
+    own_w.wait()
+    pl.semaphore_wait(barrier, n - 1 + 2)
+
+    def chain_d(o_z, cond_up, cond_dn):
+        ref = dbuf.at[at(o_z)]
+        send(cond_up, rc(ref, ref, cd_s.at[0, o_z], cd_r.at[o_z], {"fsdp": at(z + 1)}))
+        send(cond_dn, rc(ref, ref, cd_s.at[1, o_z], cd_r.at[o_z], {"fsdp": at(z - 1)}))
+        send(None, rc(ref, ref, sd_s.at[o_z], sd_r.at[o_z], SIB))
+
+    def chain_w(o_z, cond_up, cond_dn):
+        ref = wbuf.at[at(o_z), quarter]
+        send(cond_up, rc(ref, ref, cw_s.at[0, o_z], cw_r.at[o_z], {"fsdp": at(z + 1)}))
+        send(cond_dn, rc(ref, ref, cw_s.at[1, o_z], cw_r.at[o_z], {"fsdp": at(z - 1)}))
+
+    chain_d(z, upper, lower)
+    chain_w(z, upper, lower)
+    whole = wbuf.at[me]
+    send(None, rc(whole, whole, so_s, so_r, SIB))
+
+    owners = tenant_ref.shape[1]
+    block = rows // owners
+    row_at = lax.broadcasted_iota(jnp.int32, (cols, rows), 1) // block
+    want = jnp.zeros((cols, rows), jnp.int32)
+    for b in range(owners):
+        t = tenant_ref[0, b]
+        s = jnp.int32(0)
+        for k in range(slot_ref.shape[1]):
+            s = s + jnp.where(t == k, slot_ref[0, k], 0)
+        want = jnp.where(row_at == b, s, want)
+    have = lax.broadcasted_iota(jnp.int32, (cols, rows), 0) // rank
+    select = jnp.where(have == want, 2.0, 0.0).astype(f32)
+    up_hi, up_lo = halves(up_ref[...])
+    cot = cot_ref[...]
+    prod = dot_nt(jnp.concatenate([up_hi, up_lo], axis=0), cot)
+    dl_hi, dl_lo = halves((prod[:cols] + prod[cols:]) * select)
+    dl_hi32, dl_lo32 = dl_hi.astype(f32), dl_lo.astype(f32)
+    dlt = jnp.concatenate([dl_hi, dl_lo], axis=0)
+    dlc[0] = jnp.concatenate([dl_hi32, dl_lo32], axis=0).T.astype(bf16)
+    dlc[1] = jnp.concatenate([dl_lo32, dl_hi32], axis=0).T.astype(bf16)
+
+    def columns(o):
+        return pl.ds(pl.multiple_of(o * depth, depth), depth)
+
+    def grad_chunk(o):
+        g = dot_nn(dlt, tok_ref[:, columns(o)])
+        gbuf[o] = g[:cols] + g[cols:]
+
+    turn = [pick(z, v) for v in ([3, 3, 0, 0], [2, 0, 3, 1], [1, 2, 1, 2], [0, 1, 2, 3])]
+    origin = [pick(z, v) for v in ([1, 0, 3, 2], [2, 2, 1, 1], [3, 3, 0, 0])]
+
+    for t in turn:
+        grad_chunk(at(t, 1 - c))
+        send(None, rc(gbuf.at[at(t, 1 - c)], pbuf.at[t], pr_s.at[t], pr_r.at[t], SIB))
+    for t in turn:
+        grad_chunk(at(t))
+
+    def chain_g(t):
+        landed(pbuf.at[t], pr_r.at[t])
+        gbuf[at(t)] += pbuf[t]
+
+        @pl.when((t > z) & lower)
+        def _():
+            landed(rup.at[t], up_r.at[t])
+            gbuf[at(t)] += rup[t]
+
+        @pl.when((t < z) & upper)
+        def _():
+            landed(rdn.at[t], dn_r.at[t])
+            gbuf[at(t)] += rdn[t]
+
+        src = gbuf.at[at(t)]
+        send(t > z, rc(src, rup.at[t], ch_s.at[t], up_r.at[t], {"fsdp": at(z + 1)}))
+        send(t < z, rc(src, rdn.at[t], ch_s.at[t], dn_r.at[t], {"fsdp": at(z - 1)}))
+
+    def spread_w(o_z):
+        ref = wbuf.at[at(o_z), quarter]
+        send(None, rc(ref, ref, nb_s.at[0, o_z], nb_r.at[0, o_z], XN))
+        send(None, rc(ref, ref, nb_s.at[1, o_z], nb_r.at[1, o_z], YN))
+        send(None, rc(ref, ref, sb_s.at[0, o_z], sb_r.at[0, o_z], SIB))
+
+    def swap_w(o_z):
+        ref = wbuf.at[at(o_z), xq]
+        landed(ref, nb_r.at[0, o_z])
+        part = wbuf.at[at(o_z), xq, pl.ds(0, half)]
+        send(None, rc(part, part, nb_s.at[2, o_z], nb_r.at[2, o_z], YN))
+        send(None, rc(ref, ref, sb_s.at[1, o_z], sb_r.at[1, o_z], SIB))
+        ref2 = wbuf.at[at(o_z), yq]
+        landed(ref2, nb_r.at[1, o_z])
+        part2 = wbuf.at[at(o_z), yq, pl.ds(half, half)]
+        send(None, rc(part2, part2, nb_s.at[3, o_z], nb_r.at[3, o_z], XN))
+        send(None, rc(ref2, ref2, sb_s.at[2, o_z], sb_r.at[2, o_z], SIB))
+
+    def last_w(o_z):
+        landed(wbuf.at[at(o_z), dq, pl.ds(0, half)], nb_r.at[2, o_z])
+        landed(wbuf.at[at(o_z), dq, pl.ds(half, half)], nb_r.at[3, o_z])
+        ref = wbuf.at[at(o_z), dq]
+        send(None, rc(ref, ref, sb_s.at[3, o_z], sb_r.at[3, o_z], SIB))
+
+    for j in range(chips - 1):
+        o_z = origin[j]
+        landed(dbuf.at[at(o_z)], cd_r.at[o_z])
+        chain_d(o_z, (o_z < z) & upper, (o_z > z) & lower)
+        landed(wbuf.at[at(o_z), quarter], cw_r.at[o_z])
+        chain_w(o_z, (o_z < z) & upper, (o_z > z) & lower)
+        spread_w(o_z)
+        chain_g(turn[j])
+        if j > 0:
+            swap_w(origin[j - 1])
+
+    for zz in range(chips):
+        landed(dbuf.at[at(zz, 1 - c)], sd_r.at[zz])
+    lacc[...] = jnp.zeros_like(lacc)
+
+    @pl.loop(0, n)
+    def _(o):
+        lacc[...] += dot_nt(dbuf[o], tok_ref[:, columns(o)])
+
+    low_hi, low_lo = halves((lacc[:cols] + lacc[cols:]) * select)
+    lowc = jnp.concatenate([low_hi.astype(f32), low_lo.astype(f32)], axis=0).T.astype(bf16)
+    cot_t = cot.astype(f32).T.astype(bf16)
+    share = ubuf.shape[1]
+    for f in range(n):
+        ubuf[f] = dot_nn(cot_t[f * share : (f + 1) * share], lowc)
+    for i in range(1, n):
+        f = lax.rem(me + i, n)
+        send(None, rc(ubuf.at[f], urecv.at[i], ug_s.at[i], ug_r.at[i], {"fsdp": f}))
+    swap_w(origin[chips - 2])
+    acc[...] = dot_nn(lowc, jnp.concatenate([up_hi, up_hi], axis=0)) + dot_nn(
+        lowc, jnp.concatenate([up_lo, up_lo], axis=0)
+    )
+
+    def apply_w(o):
+        w = wbuf[o].reshape(depth, wbuf.shape[3])
+        acc[...] += dot_nn(tok_ref[:, columns(o)], w)
+        d2 = dbuf[o]
+        back = dot_nt(cot, w) + (dot_nn(dlc[0], d2) + dot_nn(dlc[1], d2))
+        tg_ref[:, columns(o)] = back.astype(bf16)
+
+    apply_w(me)
+    landed(wbuf.at[sib], so_r)
+    apply_w(sib)
+
+    landed(pbuf.at[z], pr_r.at[z])
+    dg_ref[...] = gbuf[me] + pbuf[z]
+
+    @pl.when(lower)
+    def _():
+        landed(rup.at[z], up_r.at[z])
+        dg_ref[...] += rup[z]
+
+    @pl.when(upper)
+    def _():
+        landed(rdn.at[z], dn_r.at[z])
+        dg_ref[...] += rdn[z]
+
+    for j in range(chips - 1):
+        o_z = origin[j]
+        last_w(o_z)
+        apply_w(at(o_z))
+        for k, q in enumerate((quarter, xq, yq, dq)):
+            landed(wbuf.at[at(o_z, 1 - c), q], sb_r.at[k, o_z])
+        apply_w(at(o_z, 1 - c))
+
+    total = ubuf[me]
+    for i in range(1, n):
+        landed(urecv.at[i], ug_r.at[i])
+        total = total + urecv[i]
+    ug_ref[...] = total
+    proj_ref[...] = acc[...].astype(bf16)
+
+    for cond, copy in sends:
+        if cond is None:
+            copy.wait_send()
+        else:
+            pl.when(cond)(copy.wait_send)
+
+
+def fused_step(chips, tokens, weight, downs, ups, tenants, slots, cotangent):
+    rows, width = tokens.shape[1:]
+    depth, out_width = weight.shape
+    slot_count, rank = downs.shape[1], downs.shape[3]
+    cols = slot_count * rank
+    n = chips * CORES
+    quarters = 4
+    share = out_width // n
+    down_t = jnp.transpose(downs[0], (0, 2, 1)).reshape(cols, depth)
+    dma = pltpu.SemaphoreType.DMA
+    vmem = pl.BlockSpec(memory_space=pltpu.VMEM)
+    smem = pl.BlockSpec(memory_space=pltpu.SMEM)
+    proj, tg, dg, ug = pl.pallas_call(
+        functools.partial(step_kernel, chips, quarters, rank),
+        out_shape=(
+            jax.ShapeDtypeStruct((rows, out_width), bf16),
+            jax.ShapeDtypeStruct((rows, width), bf16),
+            jax.ShapeDtypeStruct((cols, depth), f32),
+            jax.ShapeDtypeStruct((share, 2 * cols), f32),
+        ),
+        in_specs=[vmem, pl.BlockSpec(memory_space=pl.ANY), vmem, vmem, smem, smem, vmem],
+        out_specs=(vmem,) * 4,
+        scratch_shapes=[
+            pltpu.VMEM((n, quarters, depth // quarters, out_width), bf16),
+            pltpu.VMEM((n, 2 * cols, depth), bf16),
+            pltpu.VMEM((n, cols, depth), f32),
+            pltpu.VMEM((chips, cols, depth), f32),
+            pltpu.VMEM((chips, cols, depth), f32),
+            pltpu.VMEM((chips, cols, depth), f32),
+            pltpu.VMEM((n, share, 2 * cols), f32),
+            pltpu.VMEM((n, share, 2 * cols), f32),
+            pltpu.VMEM((2, rows, 2 * cols), bf16),
+            pltpu.VMEM((rows, out_width), f32),
+            pltpu.VMEM((2 * cols, rows), f32),
+            dma((2, chips)),
+            dma((chips,)),
+            dma((2, chips)),
+            dma((chips,)),
+            dma((chips,)),
+            dma((chips,)),
+            dma((4, chips)),
+            dma((4, chips)),
+            dma((4, chips)),
+            dma((4, chips)),
+            dma,
+            dma,
+            dma((chips,)),
+            dma((chips,)),
+            dma((chips,)),
+            dma((chips,)),
+            dma((chips,)),
+            dma((n,)),
+            dma((n,)),
+            dma,
+        ],
+        compiler_params=pltpu.CompilerParams(
+            collective_id=0, has_side_effects=True, vmem_limit_bytes=48 * 1024 * 1024
+        ),
+        cost_estimate=pl.CostEstimate(
+            flops=5 * rows * width * out_width, bytes_accessed=8 * 1024 * 1024, transcendentals=0
+        ),
+    )(
+        tokens[0],
+        weight.reshape(quarters, depth // quarters, out_width),
+        down_t,
+        ups[0].reshape(cols, out_width),
+        tenants,
+        slots,
+        cotangent[0],
+    )
+    down_gradient = jnp.transpose(dg.reshape(slot_count, rank, depth), (0, 2, 1))[None]
+    up_gradient = ug[:, :cols] + ug[:, cols:]
+    up_gradient = jnp.transpose(up_gradient.reshape(share, slot_count, rank), (1, 0, 2))[None]
+    return proj[None], tg[None], down_gradient, up_gradient
+
+
 def solution(mesh):
+    sizes = (mesh.shape["rep"], mesh.shape["fsdp"], mesh.shape["adapt"], mesh.shape["sub"])
+    body = functools.partial(fused_step, sizes[1] // CORES) if sizes == (2, 8, 2, 1) else per_device
     in_specs = (
         P("adapt", ("rep", "fsdp", "sub"), None),
         P("fsdp", None),
@@ -89,5 +471,5 @@
         P("adapt", "rep", ("fsdp", "sub"), None),
     )
     return jax.shard_map(
-        per_device, mesh=mesh, in_specs=in_specs, out_specs=out_specs, check_vma=False
-    )
+        body, mesh=mesh, in_specs=in_specs, out_specs=out_specs, check_vma=False
+    )

time: 204 us -> 85.8 us (0.42)
  waiting for transfers between devices: 165 us -> 0 us
  Pallas kernels: 0 us -> 74.2 us
  matrix products: 20.1 us -> 0 us
  between operations: 13.9 us -> 0.66 us
  local copies, waits for them, and re-layouts: 3.72 us -> 10.3 us
    all_gather x2 -> x0, waiting for transfers between devices: 113 us -> none  [the longest x1 80.3 us: per_device(): whole_weight = lax.all_gather(frozen_key_weight, 'fsdp', axis=0, tiled=True)]
    pallas_call x0 -> x1, Pallas kernels: none -> 74.2 us  [fused_step(): pl.pallas_call(functools.partial(step_kernel, chips, quarters, rank), out...]
    unnamed x5 -> x0, waiting for transfers between devices: 28 us -> none
    reduce_scatter x1 -> x0, waiting for transfers between devices: 23.8 us -> none  [per_device(): lax.psum_scatter(grad_a_local, ('fsdp', 'sub'), scatter_dimension=2, tile...]
    dot_general x8 -> x0, matrix products: 20.1 us -> none  [the longest x1 4.78 us: per_device(): jnp.dot(feats, whole_weight, preferred_element_type=jnp.float32)]
    unnamed x18 -> x17, local copies, waits for them, and re-layouts: 3.56 us -> 9.55 us
  transfers between devices with their start and end apart: 4 -> 0, of which waited for: 4 -> 0; matrix products, arithmetic and copies ran while one was open for 9% -> 0% of each run, Pallas kernels for 0% -> 0%
where the time goes in v1:
time: 85.8 us; the launch traced here: 85.2 us
  Pallas kernels  74.2 us (86%)
  local copies, waits for them, and re-layouts  10.3 us (12%)
    pallas_call x1, Pallas kernels, fused_step(): pl.pallas_call(functools.partial(step_kernel, chips, quarters, rank), out...  74.2 us
    unnamed x17, local copies, waits for them, and re-layouts  9.55 us

profile of v1, /device:TPU:0, one launch (start us, length us, event | category | flops | bytes accessed | tf_op | source)
XLA Modules:
  0.0 85.2 jit_solution(1149483169861710112)
XLA Ops:
  0.6 0.0 copy-start
  0.6 1.6 %copy-done = bf16[1,128,8192]{2,1,0:T(8,128)(2,1)S(1)} copy-done((bf16[1,128,8192]{2,1,0:T(8,128)(2,1)S(1)}, bf16[1,128,8192]{2,1,0:T(8,128)(2,1)}, u32[]{:S(2)}) %copy-start) | copy-done | bytes 2097176
  2.2 0.0 copy-start.1
  2.2 1.2 %copy-done.1 = bf16[1024,512]{1,0:T(8,128)(2,1)S(1)} copy-done((bf16[1024,512]{1,0:T(8,128)(2,1)S(1)}, bf16[1024,512]{1,0:T(8,128)(2,1)}, u32[]{:S(2)}) %copy-start.1) | copy-done | bytes 1048600
  3.5 0.0 copy-start.2
  3.5 0.9 %copy-done.2 = f32[1,4,1024,16]{2,3,1,0:T(8,128)S(1)} copy-done((f32[1,4,1024,16]{2,3,1,0:T(8,128)S(1)}, f32[1,4,1024,16]{2,3,1,0:T(8,128)}, u32[]{:S(2)}) %copy-start.2) | copy-done | bytes 262168
  4.4 0.0 copy-start.3
  4.4 0.9 %copy-done.3 = f32[1,4,16,512]{3,2,1,0:T(8,128)S(1)} copy-done((f32[1,4,16,512]{3,2,1,0:T(8,128)S(1)}, f32[1,4,16,512]{3,2,1,0:T(8,128)}, u32[]{:S(2)}) %copy-start.3) | copy-done | bytes 131096
  5.3 0.0 copy-start.4
  5.3 0.9 %copy-done.4 = bf16[1,128,512]{2,1,0:T(8,128)(2,1)S(1)} copy-done((bf16[1,128,512]{2,1,0:T(8,128)(2,1)S(1)}, bf16[1,128,512]{2,1,0:T(8,128)(2,1)}, u32[]{:S(2)}) %copy-start.4) | copy-done | bytes 131096
  6.2 0.0 copy-start.5
  6.2 0.7 copy-done.5
  6.9 0.0 copy-start.6
  6.9 0.7 copy-done.6
  7.5 74.2 %shard_map.102 = (bf16[128,512]{1,0:T(8,128)(2,1)S(1)}, bf16[128,8192]{1,0:T(8,128)(2,1)S(1)}, f32[64,1024]{1,0:T(8,128)S(1)}, f32[64,128]{1,0:T(8,128)S(1)}) custom-call(bf16[128,8192]{1,0:T(8,128)(2,1)S(1)} %bitcast.24, bf16[4,256,512]{2,1,0:T(8,128)(2,1)S(1)} %bitcast.25, f32[64,1024]{1,0:T(8,128)S(1)} %bitcast.26, f32[64,512]{1,0:T(8,128)S(1)} %bitcast.27, ...), custom_call_target="tpu_custom_call" | custom-call | flops 2684354560 | bytes 8388608 | tf_op jit(solution)/shard_map/pallas_call | solution.py:391
  81.8 0.1 slice_add_fusion
  81.8 0.7 copy.12
  82.6 0.7 copy.16
  83.2 1.3 %copy.17 = bf16[1,128,8192]{2,1,0:T(8,128)(2,1)} copy(bf16[1,128,8192]{2,1,0:T(8,128)(2,1)S(1)} %bitcast.21) | data formatting | bytes 4194304
  84.5 0.7 copy.18
Async XLA Ops:
  0.6 1.6 %copy-start = (bf16[1,128,8192]{2,1,0:T(8,128)(2,1)S(1)}, bf16[1,128,8192]{2,1,0:T(8,128)(2,1)}, u32[]{:S(2)}) copy-start(bf16[1,128,8192]{2,1,0:T(8,128)(2,1)} %param.7) | copy-start | bytes 6291460
  2.2 1.2 %copy-start.1 = (bf16[1024,512]{1,0:T(8,128)(2,1)S(1)}, bf16[1024,512]{1,0:T(8,128)(2,1)}, u32[]{:S(2)}) copy-start(bf16[1024,512]{1,0:T(8,128)(2,1)} %param.8) | copy-start | bytes 3145732
  3.5 0.9 %copy-start.2 = (f32[1,4,1024,16]{2,3,1,0:T(8,128)S(1)}, f32[1,4,1024,16]{2,3,1,0:T(8,128)}, u32[]{:S(2)}) copy-start(f32[1,4,1024,16]{2,3,1,0:T(8,128)} %param.9) | copy-start | bytes 786436
  4.4 0.9 %copy-start.3 = (f32[1,4,16,512]{3,2,1,0:T(8,128)S(1)}, f32[1,4,16,512]{3,2,1,0:T(8,128)}, u32[]{:S(2)}) copy-start(f32[1,4,16,512]{3,2,1,0:T(8,128)} %param.10) | copy-start | bytes 393220
  5.3 0.9 %copy-start.4 = (bf16[1,128,512]{2,1,0:T(8,128)(2,1)S(1)}, bf16[1,128,512]{2,1,0:T(8,128)(2,1)}, u32[]{:S(2)}) copy-start(bf16[1,128,512]{2,1,0:T(8,128)(2,1)} %param.13) | copy-start | bytes 393220
  6.2 0.7 copy-start.5
  6.9 0.7 copy-start.6

commit v2 on v1

--- a/solution.py
+++ b/solution.py
@@ -106,13 +106,13 @@
     chips,
     quarters,
     rank,
-    tok_ref,
+    tok_in,
     w_ref,
-    d_ref,
-    up_ref,
-    tenant_ref,
-    slot_ref,
-    cot_ref,
+    d_in,
+    up_in,
+    tenant_in,
+    slot_in,
+    cot_in,
     proj_ref,
     tg_ref,
     dg_ref,
@@ -148,6 +148,12 @@
     ug_s,
     ug_r,
     cp_s,
+    tok_ref,
+    d_ref,
+    up_ref,
+    tenant_ref,
+    slot_ref,
+    cot_ref,
 ):
     me = lax.axis_index("fsdp")
     a = lax.axis_index("adapt")
@@ -159,9 +165,9 @@
     xq = r * 2 + (1 - a)
     yq = (1 - r) * 2 + a
     dq = (1 - r) * 2 + (1 - a)
-    rows, width = tok_ref.shape
+    rows, width = tok_in.shape
     depth = width // n
-    cols = d_ref.shape[0]
+    cols = d_in.shape[0]
     half = wbuf.shape[2] // 2
     upper, lower = z < chips - 1, z > 0
     SIB, XN, YN = {"fsdp": sib}, {"adapt": 1 - a}, {"rep": 1 - r}
@@ -187,8 +193,22 @@
     def landed(dst, rs):
         rc(dst, dst, sb_s.at[0, 0], rs, SIB).wait_recv()
 
-    own_w = pltpu.make_async_copy(w_ref, wbuf.at[me], cp_s)
-    own_w.start()
+    fetches = [
+        pltpu.make_async_copy(src, dst, cp_s.at[i])
+        for i, (src, dst) in enumerate(
+            (
+                (w_ref, wbuf.at[me]),
+                (cot_in, cot_ref),
+                (up_in, up_ref),
+                (tenant_in, tenant_ref),
+                (slot_in, slot_ref),
+                (tok_in, tok_ref),
+                (d_in, d_ref),
+            )
+        )
+    ]
+    for fetch in fetches:
+        fetch.start()
 
     barrier = pltpu.get_barrier_semaphore()
     for i in range(1, n):
@@ -196,10 +216,7 @@
     pl.semaphore_signal(barrier, inc=1, device_id=XN, device_id_type=MESH)
     pl.semaphore_signal(barrier, inc=1, device_id=YN, device_id_type=MESH)
 
-    d_hi, d_lo = halves(d_ref[...])
-    dbuf[me, :cols] = d_hi
-    dbuf[me, cols:] = d_lo
-    own_w.wait()
+    fetches[0].wait()
     pl.semaphore_wait(barrier, n - 1 + 2)
 
     def chain_d(o_z, cond_up, cond_dn):
@@ -213,10 +230,12 @@
         send(cond_up, rc(ref, ref, cw_s.at[0, o_z], cw_r.at[o_z], {"fsdp": at(z + 1)}))
         send(cond_dn, rc(ref, ref, cw_s.at[1, o_z], cw_r.at[o_z], {"fsdp": at(z - 1)}))
 
-    chain_d(z, upper, lower)
     chain_w(z, upper, lower)
     whole = wbuf.at[me]
     send(None, rc(whole, whole, so_s, so_r, SIB))
+
+    for fetch in fetches[1:5]:
+        fetch.wait()
 
     owners = tenant_ref.shape[1]
     block = rows // owners
@@ -239,6 +258,12 @@
     dlc[0] = jnp.concatenate([dl_hi32, dl_lo32], axis=0).T.astype(bf16)
     dlc[1] = jnp.concatenate([dl_lo32, dl_hi32], axis=0).T.astype(bf16)
 
+    for fetch in fetches[5:]:
+        fetch.wait()
+    d_hi, d_lo = halves(d_ref[...])
+    dbuf[me, :cols] = d_hi
+    dbuf[me, cols:] = d_lo
+
     def columns(o):
         return pl.ds(pl.multiple_of(o * depth, depth), depth)
 
@@ -255,10 +280,11 @@
     for t in turn:
         grad_chunk(at(t))
 
-    def chain_g(t):
+    def pair_g(t):
         landed(pbuf.at[t], pr_r.at[t])
         gbuf[at(t)] += pbuf[t]
 
+    def gather_g(t):
         @pl.when((t > z) & lower)
         def _():
             landed(rup.at[t], up_r.at[t])
@@ -269,9 +295,11 @@
             landed(rdn.at[t], dn_r.at[t])
             gbuf[at(t)] += rdn[t]
 
+    def send_g(t, cond):
         src = gbuf.at[at(t)]
-        send(t > z, rc(src, rup.at[t], ch_s.at[t], up_r.at[t], {"fsdp": at(z + 1)}))
-        send(t < z, rc(src, rdn.at[t], ch_s.at[t], dn_r.at[t], {"fsdp": at(z - 1)}))
+        above, below = (t > z, t < z) if cond is None else (cond & (t > z), cond & (t < z))
+        send(above, rc(src, rup.at[t], ch_s.at[t], up_r.at[t], {"fsdp": at(z + 1)}))
+        send(below, rc(src, rdn.at[t], ch_s.at[t], dn_r.at[t], {"fsdp": at(z - 1)}))
 
     def spread_w(o_z):
         ref = wbuf.at[at(o_z), quarter]
@@ -297,16 +325,40 @@
         ref = wbuf.at[at(o_z), dq]
         send(None, rc(ref, ref, sb_s.at[3, o_z], sb_r.at[3, o_z], SIB))
 
-    for j in range(chips - 1):
+    def take_w(j):
+        o_z = origin[j]
+        landed(wbuf.at[at(o_z), quarter], cw_r.at[o_z])
+        chain_w(o_z, (o_z < z) & upper, (o_z > z) & lower)
+        spread_w(o_z)
+
+    def take_d(j):
         o_z = origin[j]
         landed(dbuf.at[at(o_z)], cd_r.at[o_z])
         chain_d(o_z, (o_z < z) & upper, (o_z > z) & lower)
-        landed(wbuf.at[at(o_z), quarter], cw_r.at[o_z])
-        chain_w(o_z, (o_z < z) & upper, (o_z > z) & lower)
-        spread_w(o_z)
-        chain_g(turn[j])
-        if j > 0:
-            swap_w(origin[j - 1])
+
+    ends = (z == 0) | (z == chips - 1)
+    take_w(0)
+    pair_g(turn[0])
+    send_g(turn[0], ends)
+    take_w(1)
+    chain_d(z, upper, lower)
+    swap_w(origin[0])
+    take_w(2)
+    gather_g(turn[0])
+    send_g(turn[0], jnp.logical_not(ends))
+    swap_w(origin[1])
+    take_d(0)
+    pair_g(turn[1])
+    gather_g(turn[1])
+    send_g(turn[1], None)
+    swap_w(origin[2])
+    take_d(1)
+    pair_g(turn[2])
+    gather_g(turn[2])
+    send_g(turn[2], None)
+    for j in range(chips - 1):
+        last_w(origin[j])
+    take_d(2)
 
     for zz in range(chips):
         landed(dbuf.at[at(zz, 1 - c)], sd_r.at[zz])
@@ -325,7 +377,6 @@
     for i in range(1, n):
         f = lax.rem(me + i, n)
         send(None, rc(ubuf.at[f], urecv.at[i], ug_s.at[i], ug_r.at[i], {"fsdp": f}))
-    swap_w(origin[chips - 2])
     acc[...] = dot_nn(lowc, jnp.concatenate([up_hi, up_hi], axis=0)) + dot_nn(
         lowc, jnp.concatenate([up_lo, up_lo], axis=0)
     )
@@ -341,6 +392,13 @@
     landed(wbuf.at[sib], so_r)
     apply_w(sib)
 
+    for j in range(chips - 1):
+        o_z = origin[j]
+        apply_w(at(o_z))
+        for k, q in enumerate((quarter, xq, yq, dq)):
+            landed(wbuf.at[at(o_z, 1 - c), q], sb_r.at[k, o_z])
+        apply_w(at(o_z, 1 - c))
+
     landed(pbuf.at[z], pr_r.at[z])
     dg_ref[...] = gbuf[me] + pbuf[z]
 
@@ -354,19 +412,12 @@
         landed(rdn.at[z], dn_r.at[z])
         dg_ref[...] += rdn[z]
 
-    for j in range(chips - 1):
-        o_z = origin[j]
-        last_w(o_z)
-        apply_w(at(o_z))
-        for k, q in enumerate((quarter, xq, yq, dq)):
-            landed(wbuf.at[at(o_z, 1 - c), q], sb_r.at[k, o_z])
-        apply_w(at(o_z, 1 - c))
-
     total = ubuf[me]
     for i in range(1, n):
         landed(urecv.at[i], ug_r.at[i])
         total = total + urecv[i]
-    ug_ref[...] = total
+    total = total.T
+    ug_ref[...] = total[:cols] + total[cols:]
     proj_ref[...] = acc[...].astype(bf16)
 
     for cond, copy in sends:
@@ -374,6 +425,34 @@
             copy.wait_send()
         else:
             pl.when(cond)(copy.wait_send)
+
+
+PIECES = 8
+
+
+def write_kernel(*refs):
+    ins, outs, held, sems = refs[:4], refs[4:8], refs[8:12], refs[12]
+    ways = []
+    for i in range(4):
+        rows = ins[i].shape[0]
+        pieces = PIECES if i == 1 else 1
+        size = rows // pieces
+        for p in range(pieces):
+            part = pl.ds(p * size, size)
+            k = len(ways)
+            ways.append(
+                (
+                    pltpu.make_async_copy(ins[i].at[part], held[i].at[part], sems.at[0, k]),
+                    pltpu.make_async_copy(held[i].at[part], outs[i].at[part], sems.at[1, k]),
+                )
+            )
+    for way in ways:
+        way[0].start()
+    for way in ways:
+        way[0].wait()
+        way[1].start()
+    for way in ways:
+        way[1].wait()
 
 
 def fused_step(chips, tokens, weight, downs, ups, tenants, slots, cotangent):
@@ -387,16 +466,16 @@
     down_t = jnp.transpose(downs[0], (0, 2, 1)).reshape(cols, depth)
     dma = pltpu.SemaphoreType.DMA
     vmem = pl.BlockSpec(memory_space=pltpu.VMEM)
-    smem = pl.BlockSpec(memory_space=pltpu.SMEM)
+    hbm = pl.BlockSpec(memory_space=pltpu.HBM)
     proj, tg, dg, ug = pl.pallas_call(
         functools.partial(step_kernel, chips, quarters, rank),
         out_shape=(
             jax.ShapeDtypeStruct((rows, out_width), bf16),
             jax.ShapeDtypeStruct((rows, width), bf16),
             jax.ShapeDtypeStruct((cols, depth), f32),
-            jax.ShapeDtypeStruct((share, 2 * cols), f32),
+            jax.ShapeDtypeStruct((cols, share), f32),
         ),
-        in_specs=[vmem, pl.BlockSpec(memory_space=pl.ANY), vmem, vmem, smem, smem, vmem],
+        in_specs=[hbm] * 7,
         out_specs=(vmem,) * 4,
         scratch_shapes=[
             pltpu.VMEM((n, quarters, depth // quarters, out_width), bf16),
@@ -429,10 +508,16 @@
             dma((chips,)),
             dma((n,)),
             dma((n,)),
-            dma,
+            dma((7,)),
+            pltpu.VMEM((rows, width), bf16),
+            pltpu.VMEM((cols, depth), f32),
+            pltpu.VMEM((cols, out_width), f32),
+            pltpu.SMEM(tenants.shape, jnp.int32),
+            pltpu.SMEM(slots.shape, jnp.int32),
+            pltpu.VMEM((rows, out_width), bf16),
         ],
         compiler_params=pltpu.CompilerParams(
-            collective_id=0, has_side_effects=True, vmem_limit_bytes=48 * 1024 * 1024
+            collective_id=0, has_side_effects=True, vmem_limit_bytes=63 * 1024 * 1024
         ),
         cost_estimate=pl.CostEstimate(
             flops=5 * rows * width * out_width, bytes_accessed=8 * 1024 * 1024, transcendentals=0
@@ -446,9 +531,18 @@
         slots,
         cotangent[0],
     )
+    proj, tg, dg, ug = pl.pallas_call(
+        write_kernel,
+        out_shape=tuple(jax.ShapeDtypeStruct(x.shape, x.dtype) for x in (proj, tg, dg, ug)),
+        in_specs=[pl.BlockSpec(memory_space=pl.ANY)] * 4,
+        out_specs=(hbm,) * 4,
+        scratch_shapes=[pltpu.VMEM(x.shape, x.dtype) for x in (proj, tg, dg, ug)]
+        + [dma((2, PIECES + 3))],
+        compiler_params=pltpu.CompilerParams(vmem_limit_bytes=63 * 1024 * 1024),
+        cost_estimate=pl.CostEstimate(flops=0, bytes_accessed=4 * rows * width, transcendentals=0),
+    )(proj, tg, dg, ug)
     down_gradient = jnp.transpose(dg.reshape(slot_count, rank, depth), (0, 2, 1))[None]
-    up_gradient = ug[:, :cols] + ug[:, cols:]
-    up_gradient = jnp.transpose(up_gradient.reshape(share, slot_count, rank), (1, 0, 2))[None]
+    up_gradient = jnp.transpose(ug.reshape(slot_count, rank, share), (0, 2, 1))[None]
     return proj[None], tg[None], down_gradient, up_gradient
 
 

time: 85.8 us -> 65.5 us (0.76)
  Pallas kernels: 74.2 us -> 63.7 us
  local copies, waits for them, and re-layouts: 10.3 us -> 0 us
    pallas_call x1, Pallas kernels: 74.2 us -> 61.1 us  [fused_step(): pl.pallas_call(functools.partial(step_kernel, chips, quarters, rank), out...]
    unnamed x17 -> x0, local copies, waits for them, and re-layouts: 9.55 us -> none
    pallas_call x0 -> x1, Pallas kernels: none -> 2.61 us  [fused_step(): pl.pallas_call(write_kernel, out_shape=tuple((jax.ShapeDtypeStruct(x.shap...]
where the time goes in v2:
time: 65.5 us; the launch traced here: 64.3 us
  Pallas kernels  63.7 us (97%)
    pallas_call x1, Pallas kernels, fused_step(): pl.pallas_call(functools.partial(step_kernel, chips, quarters, rank), out...  61.1 us
    pallas_call x1, Pallas kernels, fused_step(): pl.pallas_call(write_kernel, out_shape=tuple((jax.ShapeDtypeStruct(x.shap...  2.61 us

profile of v2, /device:TPU:0, one launch (start us, length us, event | category | flops | bytes accessed | tf_op | source)
XLA Modules:
  0.0 64.3 jit_solution(17963315174528040353)
XLA Ops:
  0.6 61.1 %shard_map.102 = (bf16[128,512]{1,0:T(8,128)(2,1)}, bf16[128,8192]{1,0:T(8,128)(2,1)}, f32[64,1024]{1,0:T(8,128)}, f32[64,64]{1,0:T(8,128)}) custom-call(bf16[128,8192]{1,0:T(8,128)(2,1)} %bitcast.21, bf16[4,256,512]{2,1,0:T(8,128)(2,1)} %bitcast.23, f32[64,1024]{1,0:T(8,128)} %bitcast.24, f32[64,512]{1,0:T(8,128)} %bitcast.26, s32[1,2]{1,0:T(1,128)} %tenant_in.1, ...), custom_call_target="tpu_custom_call" | custom-call | flops 2684354560 | bytes 8388608 | tf_op jit(solution)/shard_map/pallas_call | solution.py:470
  61.7 2.6 %shard_map.103 = (bf16[128,512]{1,0:T(8,128)(2,1)}, bf16[128,8192]{1,0:T(8,128)(2,1)}, f32[64,1024]{1,0:T(8,128)}, f32[64,64]{1,0:T(8,128)}) custom-call(bf16[128,512]{1,0:T(8,128)(2,1)} %get-tuple-element.12.refs_0_, bf16[128,8192]{1,0:T(8,128)(2,1)} %get-tuple-element.13.refs_1_, f32[64,1024]{1,0:T(8,128)} %get-tuple-element.14.refs_2_, ...), custom_call_target="tpu_custom_call" | custom-call | bytes 4194304 | tf_op jit(solution)/shard_map/pallas_call | solution.py:534

commit v3 on v2

--- a/solution.py
+++ b/solution.py
@@ -114,7 +114,7 @@
     slot_in,
     cot_in,
     proj_ref,
-    tg_ref,
+    tg_out,
     dg_ref,
     ug_ref,
     wbuf,
@@ -154,6 +154,9 @@
     tenant_ref,
     slot_ref,
     cot_ref,
+    tgf,
+    tg_ref,
+    tg_s,
 ):
     me = lax.axis_index("fsdp")
     a = lax.axis_index("adapt")
@@ -277,6 +280,7 @@
     for t in turn:
         grad_chunk(at(t, 1 - c))
         send(None, rc(gbuf.at[at(t, 1 - c)], pbuf.at[t], pr_s.at[t], pr_r.at[t], SIB))
+    chain_d(z, upper, lower)
     for t in turn:
         grad_chunk(at(t))
 
@@ -336,37 +340,61 @@
         landed(dbuf.at[at(o_z)], cd_r.at[o_z])
         chain_d(o_z, (o_z < z) & upper, (o_z > z) & lower)
 
+    def base_w(o):
+        w = wbuf[o].reshape(depth, wbuf.shape[3])
+        acc[...] += dot_nn(tok_ref[:, columns(o)], w)
+        tgf[:, columns(o)] = dot_nt(cot_ref[...], w)
+
+    def low_d(o):
+        lacc[...] += dot_nt(dbuf[o], tok_ref[:, columns(o)])
+
+    def tg_copy(o):
+        return pltpu.make_async_copy(tg_ref.at[:, columns(o)], tg_out.at[:, columns(o)], tg_s.at[o])
+
+    def back_d(o):
+        d2 = dbuf[o]
+        back = tgf[:, columns(o)] + (dot_nn(dlc[0], d2) + dot_nn(dlc[1], d2))
+        tg_ref[:, columns(o)] = back.astype(bf16)
+        tg_copy(o).start()
+
     ends = (z == 0) | (z == chips - 1)
+    inner = jnp.logical_not(ends)
+    acc[...] = jnp.zeros_like(acc)
+    lacc[...] = jnp.zeros_like(lacc)
     take_w(0)
     pair_g(turn[0])
     send_g(turn[0], ends)
     take_w(1)
-    chain_d(z, upper, lower)
+    base_w(me)
     swap_w(origin[0])
     take_w(2)
     gather_g(turn[0])
-    send_g(turn[0], jnp.logical_not(ends))
+    send_g(turn[0], inner)
+    low_d(me)
     swap_w(origin[1])
     take_d(0)
+    low_d(at(origin[0]))
+    landed(wbuf.at[sib], so_r)
+    base_w(sib)
     pair_g(turn[1])
     gather_g(turn[1])
     send_g(turn[1], None)
     swap_w(origin[2])
     take_d(1)
+    low_d(at(origin[1]))
     pair_g(turn[2])
+    send_g(turn[2], ends)
+    last_w(origin[0])
+    base_w(at(origin[0]))
+    last_w(origin[1])
+    take_d(2)
     gather_g(turn[2])
-    send_g(turn[2], None)
-    for j in range(chips - 1):
-        last_w(origin[j])
-    take_d(2)
-
-    for zz in range(chips):
+    send_g(turn[2], inner)
+    base_w(at(origin[1]))
+    low_d(at(origin[2]))
+    for zz in [z] + origin:
         landed(dbuf.at[at(zz, 1 - c)], sd_r.at[zz])
-    lacc[...] = jnp.zeros_like(lacc)
-
-    @pl.loop(0, n)
-    def _(o):
-        lacc[...] += dot_nt(dbuf[o], tok_ref[:, columns(o)])
+        low_d(at(zz, 1 - c))
 
     low_hi, low_lo = halves((lacc[:cols] + lacc[cols:]) * select)
     lowc = jnp.concatenate([low_hi.astype(f32), low_lo.astype(f32)], axis=0).T.astype(bf16)
@@ -377,27 +405,19 @@
     for i in range(1, n):
         f = lax.rem(me + i, n)
         send(None, rc(ubuf.at[f], urecv.at[i], ug_s.at[i], ug_r.at[i], {"fsdp": f}))
-    acc[...] = dot_nn(lowc, jnp.concatenate([up_hi, up_hi], axis=0)) + dot_nn(
+    last_w(origin[2])
+    acc[...] += dot_nn(lowc, jnp.concatenate([up_hi, up_hi], axis=0)) + dot_nn(
         lowc, jnp.concatenate([up_lo, up_lo], axis=0)
     )
-
-    def apply_w(o):
-        w = wbuf[o].reshape(depth, wbuf.shape[3])
-        acc[...] += dot_nn(tok_ref[:, columns(o)], w)
-        d2 = dbuf[o]
-        back = dot_nt(cot, w) + (dot_nn(dlc[0], d2) + dot_nn(dlc[1], d2))
-        tg_ref[:, columns(o)] = back.astype(bf16)
-
-    apply_w(me)
-    landed(wbuf.at[sib], so_r)
-    apply_w(sib)
-
-    for j in range(chips - 1):
-        o_z = origin[j]
-        apply_w(at(o_z))
+    for o in (me, sib, at(origin[0]), at(origin[1])):
+        back_d(o)
+    base_w(at(origin[2]))
+    back_d(at(origin[2]))
+    for o_z in origin:
         for k, q in enumerate((quarter, xq, yq, dq)):
             landed(wbuf.at[at(o_z, 1 - c), q], sb_r.at[k, o_z])
-        apply_w(at(o_z, 1 - c))
+        base_w(at(o_z, 1 - c))
+        back_d(at(o_z, 1 - c))
 
     landed(pbuf.at[z], pr_r.at[z])
     dg_ref[...] = gbuf[me] + pbuf[z]
@@ -420,6 +440,8 @@
     ug_ref[...] = total[:cols] + total[cols:]
     proj_ref[...] = acc[...].astype(bf16)
 
+    for o in range(n):
+        tg_copy(o).wait()
     for cond, copy in sends:
         if cond is None:
             copy.wait_send()
@@ -476,7 +498,7 @@
             jax.ShapeDtypeStruct((cols, share), f32),
         ),
         in_specs=[hbm] * 7,
-        out_specs=(vmem,) * 4,
+        out_specs=(vmem, hbm, vmem, vmem),
         scratch_shapes=[
             pltpu.VMEM((n, quarters, depth // quarters, out_width), bf16),
             pltpu.VMEM((n, 2 * cols, depth), bf16),
@@ -515,6 +537,9 @@
             pltpu.SMEM(tenants.shape, jnp.int32),
             pltpu.SMEM(slots.shape, jnp.int32),
             pltpu.VMEM((rows, out_width), bf16),
+            pltpu.VMEM((rows, width), f32),
+            pltpu.VMEM((rows, width), bf16),
+            dma((n,)),
         ],
         compiler_params=pltpu.CompilerParams(
             collective_id=0, has_side_effects=True, vmem_limit_bytes=63 * 1024 * 1024

time: 65.5 us -> 62.9 us (0.960); the launches traced: 64.3 us -> 62.7 us
  Pallas kernels: 63.7 us -> 62.1 us
    pallas_call x1, Pallas kernels: 61.1 us -> 59.5 us  [fused_step(): pl.pallas_call(functools.partial(step_kernel, chips, quarters, rank), out...]
where the time goes in v3:
time: 62.9 us; the launch traced here: 62.7 us
  Pallas kernels  62.1 us (99%)
  between operations  0.64 us (1%)
    pallas_call x1, Pallas kernels, fused_step(): pl.pallas_call(functools.partial(step_kernel, chips, quarters, rank), out...  59.5 us
    pallas_call x1, Pallas kernels, fused_step(): pl.pallas_call(write_kernel, out_shape=tuple((jax.ShapeDtypeStruct(x.shap...  2.61 us

profile of v3, /device:TPU:0, one launch (start us, length us, event | category | flops | bytes accessed | tf_op | source)
XLA Modules:
  0.0 62.7 jit_solution(13583976491525181832)
XLA Ops:
  0.6 59.5 %shard_map.102 = (bf16[128,512]{1,0:T(8,128)(2,1)}, bf16[128,8192]{1,0:T(8,128)(2,1)}, f32[64,1024]{1,0:T(8,128)}, f32[64,64]{1,0:T(8,128)}) custom-call(bf16[128,8192]{1,0:T(8,128)(2,1)} %bitcast.21, bf16[4,256,512]{2,1,0:T(8,128)(2,1)} %bitcast.23, f32[64,1024]{1,0:T(8,128)} %bitcast.24, f32[64,512]{1,0:T(8,128)} %bitcast.26, s32[1,2]{1,0:T(1,128)} %tenant_in.1, ...), custom_call_target="tpu_custom_call" | custom-call | flops 2684354560 | bytes 8388608 | tf_op jit(solution)/shard_map/pallas_call | solution.py:492
  60.1 2.6 %shard_map.103 = (bf16[128,512]{1,0:T(8,128)(2,1)}, bf16[128,8192]{1,0:T(8,128)(2,1)}, f32[64,1024]{1,0:T(8,128)}, f32[64,64]{1,0:T(8,128)}) custom-call(bf16[128,512]{1,0:T(8,128)(2,1)} %get-tuple-element.12.refs_0_, bf16[128,8192]{1,0:T(8,128)(2,1)} %get-tuple-element.13.refs_1_, f32[64,1024]{1,0:T(8,128)} %get-tuple-element.14.refs_2_, ...), custom_call_target="tpu_custom_call" | custom-call | bytes 4194304 | tf_op jit(solution)/shard_map/pallas_call | solution.py:559

commit v4 on v3

--- a/solution.py
+++ b/solution.py
@@ -399,9 +399,12 @@
     low_hi, low_lo = halves((lacc[:cols] + lacc[cols:]) * select)
     lowc = jnp.concatenate([low_hi.astype(f32), low_lo.astype(f32)], axis=0).T.astype(bf16)
     cot_t = cot.astype(f32).T.astype(bf16)
-    share = ubuf.shape[1]
+    fold = ubuf.shape[1]
+    share = 2 * fold
     for f in range(n):
-        ubuf[f] = dot_nn(cot_t[f * share : (f + 1) * share], lowc)
+        u = dot_nn(cot_t[f * share : (f + 1) * share], lowc)
+        u = u[:, :cols] + u[:, cols:]
+        ubuf[f] = jnp.concatenate([u[:fold], u[fold:]], axis=1)
     for i in range(1, n):
         f = lax.rem(me + i, n)
         send(None, rc(ubuf.at[f], urecv.at[i], ug_s.at[i], ug_r.at[i], {"fsdp": f}))
@@ -436,8 +439,8 @@
     for i in range(1, n):
         landed(urecv.at[i], ug_r.at[i])
         total = total + urecv[i]
-    total = total.T
-    ug_ref[...] = total[:cols] + total[cols:]
+    total = jnp.concatenate([total[:, :cols], total[:, cols:]], axis=0)
+    ug_ref[...] = total.T
     proj_ref[...] = acc[...].astype(bf16)
 
     for o in range(n):
@@ -506,8 +509,8 @@
             pltpu.VMEM((chips, cols, depth), f32),
             pltpu.VMEM((chips, cols, depth), f32),
             pltpu.VMEM((chips, cols, depth), f32),
-            pltpu.VMEM((n, share, 2 * cols), f32),
-            pltpu.VMEM((n, share, 2 * cols), f32),
+            pltpu.VMEM((n, share // 2, 2 * cols), f32),
+            pltpu.VMEM((n, share // 2, 2 * cols), f32),
             pltpu.VMEM((2, rows, 2 * cols), bf16),
             pltpu.VMEM((rows, out_width), f32),
             pltpu.VMEM((2 * cols, rows), f32),

time: 62.9 us -> 61.9 us (0.984)
  Pallas kernels: 62.1 us -> 61.1 us
    pallas_call x1, Pallas kernels: 59.5 us -> 58.5 us  [fused_step(): pl.pallas_call(functools.partial(step_kernel, chips, quarters, rank), out...]
where the time goes in v4:
time: 61.9 us; the launch traced here: 61.8 us
  Pallas kernels  61.1 us (99%)
  between operations  0.64 us (1%)
    pallas_call x1, Pallas kernels, fused_step(): pl.pallas_call(functools.partial(step_kernel, chips, quarters, rank), out...  58.5 us
    pallas_call x1, Pallas kernels, fused_step(): pl.pallas_call(write_kernel, out_shape=tuple((jax.ShapeDtypeStruct(x.shap...  2.61 us

profile of v4, /device:TPU:0, one launch (start us, length us, event | category | flops | bytes accessed | tf_op | source)
XLA Modules:
  0.0 61.8 jit_solution(13792497883328032063)
XLA Ops:
  0.6 58.5 %shard_map.102 = (bf16[128,512]{1,0:T(8,128)(2,1)}, bf16[128,8192]{1,0:T(8,128)(2,1)}, f32[64,1024]{1,0:T(8,128)}, f32[64,64]{1,0:T(8,128)}) custom-call(bf16[128,8192]{1,0:T(8,128)(2,1)} %bitcast.21, bf16[4,256,512]{2,1,0:T(8,128)(2,1)} %bitcast.23, f32[64,1024]{1,0:T(8,128)} %bitcast.24, f32[64,512]{1,0:T(8,128)} %bitcast.26, s32[1,2]{1,0:T(1,128)} %tenant_in.1, ...), custom_call_target="tpu_custom_call" | custom-call | flops 2684354560 | bytes 8388608 | tf_op jit(solution)/shard_map/pallas_call | solution.py:495
  59.2 2.6 %shard_map.103 = (bf16[128,512]{1,0:T(8,128)(2,1)}, bf16[128,8192]{1,0:T(8,128)(2,1)}, f32[64,1024]{1,0:T(8,128)}, f32[64,64]{1,0:T(8,128)}) custom-call(bf16[128,512]{1,0:T(8,128)(2,1)} %get-tuple-element.12.refs_0_, bf16[128,8192]{1,0:T(8,128)(2,1)} %get-tuple-element.13.refs_1_, f32[64,1024]{1,0:T(8,128)} %get-tuple-element.14.refs_2_, ...), custom_call_target="tpu_custom_call" | custom-call | bytes 4194304 | tf_op jit(solution)/shard_map/pallas_call | solution.py:562
